TPU v7x, 128 devices: a whole 4x4x4 slice. The times are simulated.
128 devices in a mesh: traj: 8 (over x, core), tm: 16 (over y, z).
Axes of the slice: x: 4, y: 4, z: 4, core: 2. Of those that a mesh axis runs over, the one named last changes fastest.
Arguments:
- frames: bfloat16 [8, 4096, 4096], P('traj', 'tm'), may hold values from -60 to 60
- w_in: bfloat16 [4096, 512], replicated, may hold values from -0.0625 to 0.0625
- b_in: float32 [512], replicated, may hold values from -3 to 3
- w_conv: bfloat16 [3, 1024, 512], replicated, may hold values from -0.5 to 0.5
- b_conv: float32 [3, 512], replicated, may hold values from -3 to 3
Outputs:
- score: float32 [], replicated
- grad_w_in: float32 [4096, 512], replicated
- grad_b_in: float32 [512], replicated
- grad_w_conv: float32 [3, 1024, 512], replicated
- grad_b_conv: float32 [3, 512], replicated
All inputs are finite; a program needn't handle non-finite values.
Results may differ from a plain program's by a relative error of at most 0.012.
Values may be sent and summed in bfloat16 or wider, within the bound.
No kernel may reach another device: no remote copies, remote signals or barrier semaphores. Data moves between devices by JAX's collectives and lax.ppermute only.
A program may use at most 128 MiB of HBM per device.

v0:
```python
import jax
import jax.numpy as jnp
from jax import lax
from jax.sharding import PartitionSpec as P

NL = 3
NS_IT = 2
LAG = 16
RIDGE = 0.0001


def from_behind(value, axis, steps):
    count = lax.axis_size(axis)
    initial, last = (max(0, -steps), min(count, count - steps))
    return lax.ppermute(value, axis, [(source, source + steps) for source in range(initial, last)])


def matmul_hi(first_mat, second_mat):
    return jnp.dot(
        first_mat, second_mat, precision=lax.Precision.HIGHEST, preferred_element_type=jnp.float32
    )


def gram_hi(first_mat, second_mat):
    return lax.dot_general(
        first_mat,
        second_mat,
        (((0,), (0,)), ((), ())),
        precision=lax.Precision.HIGHEST,
        preferred_element_type=jnp.float32,
    )


def inv_sqrt(matrix):
    unit = jnp.eye(matrix.shape[0], dtype=jnp.float32)
    shifted = matrix + RIDGE * unit
    norm_scale = jnp.sqrt(jnp.sum(shifted * shifted))
    approx = shifted / norm_scale
    inverse = unit
    for sweep in range(NS_IT):
        mixing = 1.5 * unit - 0.5 * matmul_hi(inverse, approx)
        approx = matmul_hi(approx, mixing)
        inverse = matmul_hi(mixing, inverse)
    return inverse / jnp.sqrt(norm_scale)


def vamp_score(cov_early, cov_cross, cov_later):
    koopman = matmul_hi(matmul_hi(inv_sqrt(cov_early), cov_cross), inv_sqrt(cov_later))
    return 1.0 + jnp.sum(koopman * koopman)


def per_device(frames, w_in, b_in, w_conv, b_conv):
    frames = frames[0]
    row_count, feature_dim = frames.shape
    channels = w_in.shape[1]
    segment = lax.axis_index("tm")
    segments = lax.axis_size("tm")
    stored = []
    squash0 = jnp.tanh(jnp.dot(frames, w_in, preferred_element_type=jnp.float32) + b_in)
    hidden = squash0.astype(jnp.bfloat16)
    for layer_idx in range(NL):
        dilation = 2**layer_idx
        history = from_behind(hidden[row_count - dilation :], "tm", 1)
        joined = jnp.concatenate(
            [hidden, jnp.concatenate([history, hidden[: row_count - dilation]], axis=0)], axis=1
        )
        squashed = jnp.tanh(
            jnp.dot(joined, w_conv[layer_idx], preferred_element_type=jnp.float32)
            + b_conv[layer_idx]
        )
        stored.append((joined, squashed))
        hidden = (hidden.astype(jnp.float32) + squashed).astype(jnp.bfloat16)
    upcoming = from_behind(hidden[:LAG], "tm", -1)
    is_last = segment == segments - 1
    row_ids = jnp.arange(row_count)
    pair_mask = jnp.where(jnp.logical_and(is_last, row_ids >= row_count - LAG), 0.0, 1.0)[
        :, None
    ].astype(jnp.float32)
    early_rows = hidden.astype(jnp.float32) * pair_mask
    later_rows = jnp.concatenate([hidden[LAG:], upcoming], axis=0).astype(jnp.float32) * pair_mask
    pair_count = lax.axis_size("traj") * (row_count * segments - LAG)
    totals = lax.psum((jnp.sum(early_rows, axis=0), jnp.sum(later_rows, axis=0)), ("traj", "tm"))
    centred_early = (early_rows - totals[0] / pair_count) * pair_mask
    centred_later = (later_rows - totals[1] / pair_count) * pair_mask
    moments = lax.psum(
        (
            gram_hi(centred_early, centred_early),
            gram_hi(centred_early, centred_later),
            gram_hi(centred_later, centred_later),
        ),
        ("traj", "tm"),
    )
    cov_early = moments[0] / pair_count
    cov_cross = moments[1] / pair_count
    cov_later = moments[2] / pair_count
    score, pullback = jax.vjp(vamp_score, cov_early, cov_cross, cov_later)
    grad_early, grad_cross, grad_later = pullback(jnp.ones_like(score))
    dearly = (
        matmul_hi(centred_early, grad_early + grad_early.T) + matmul_hi(centred_later, grad_cross.T)
    ) / pair_count
    dlater = (
        matmul_hi(centred_early, grad_cross) + matmul_hi(centred_later, grad_later + grad_later.T)
    ) / pair_count
    arrived = from_behind(dlater[row_count - LAG :].astype(jnp.bfloat16), "tm", 1).astype(
        jnp.float32
    )
    hidden_grad = dearly + jnp.concatenate([arrived, dlater[: row_count - LAG]], axis=0)
    weight_grads = []
    bias_grads = []
    for layer_idx in reversed(range(NL)):
        dilation = 2**layer_idx
        joined, squashed = stored[layer_idx]
        pre_grad = (hidden_grad * (1.0 - squashed * squashed)).astype(jnp.bfloat16)
        weight_grads.insert(
            0,
            lax.dot_general(
                joined, pre_grad, (((0,), (0,)), ((), ())), preferred_element_type=jnp.float32
            ),
        )
        bias_grads.insert(0, jnp.sum(pre_grad.astype(jnp.float32), axis=0))
        input_grad = lax.dot_general(
            pre_grad,
            w_conv[layer_idx],
            (((1,), (1,)), ((), ())),
            preferred_element_type=jnp.float32,
        )
        carried = from_behind(input_grad[:dilation, channels:], "tm", -1)
        hidden_grad = (
            hidden_grad
            + input_grad[:, :channels]
            + jnp.concatenate([input_grad[dilation:, channels:], carried], axis=0)
        )
    pre_grad0 = (hidden_grad * (1.0 - squash0 * squash0)).astype(jnp.bfloat16)
    local_b_in = jnp.sum(pre_grad0.astype(jnp.float32), axis=0)
    stacked_w = jnp.stack(weight_grads)
    stacked_b = jnp.stack(bias_grads)
    local_w_in = lax.dot_general(
        frames, pre_grad0, (((0,), (0,)), ((), ())), preferred_element_type=jnp.float32
    )
    grad_w_in, grad_b_in, grad_w_conv, grad_b_conv = lax.psum(
        (local_w_in, local_b_in, stacked_w, stacked_b), ("traj", "tm")
    )
    return (score, grad_w_in, grad_b_in, grad_w_conv, grad_b_conv)


def solution(mesh):
    return jax.shard_map(
        per_device,
        mesh=mesh,
        in_specs=(P("traj", "tm", None), P(), P(), P(), P()),
        out_specs=(P(), P(), P(), P(), P()),
        check_vma=False,
    )
```

profile of v0, /device:TPU:1, one launch (start us, length us, event | category | flops | bytes accessed | tf_op | source)
XLA Modules:
  0.0 631.7 jit_solution(18159884056216987852)
XLA Ops:
  7.2 1.5 copy-done
  8.8 4.4 fusion.96
  13.2 4.4 collective-permute-start
  19.5 3.6 collective-permute-start.1
  25.1 3.6 collective-permute-start.2
  29.5 2.5 add_convert_fusion
  32.0 1.3 collective-permute-start.3
  33.3 3.4 collective-permute-done.3
  36.9 75.7 %all-reduce.1 = (f32[512]{0:T(512)S(1)}, f32[512]{0:T(512)S(1)}) all-reduce(f32[512]{0:T(512)S(1)} %get-tuple-element.11, f32[512]{0:T(512)S(1)} %get-tuple-element.10), channel_id=1, replica_groups=mesh['traj'=8,'tm'=16] {'traj','tm'}, use_global_device_ids=true, to_apply=%region_5.6 | all-reduce | flops 1024 | bytes 8192 | tf_op jit(solution)/shard_map/psum | solution.py:82
  112.6 2.2 fusion.62
  114.8 2.2 fusion.57
  117.1 2.2 fusion.56
  119.6 150.6 %all-reduce.9.cloned.1.call-done = (f32[512,512]{1,0:T(8,128)}, f32[512,512]{1,0:T(8,128)}, f32[512,512]{1,0:T(8,128)}) async-done(((f32[512,512]{1,0:T(8,128)}, f32[512,512]{1,0:T(8,128)}, f32[512,512]{1,0:T(8,128)}), (f32[512,512]{1,0:T(8,128)}, f32[512,512]{1,0:T(8,128)}, f32[512,512]{1,0:T(8,128)})) %all-reduce.9.cloned.1.call-update) | async-done | bytes 3145744 | tf_op jit(solution)/shard_map/psum | solution.py:85
  270.1 2.1 multiply_reduce_fusion.6
  272.9 2.5 select_subtract_fusion.3
  276.4 2.9 fusion.90
  279.4 2.1 multiply_reduce_fusion.5
  282.2 2.5 select_subtract_fusion.1
  284.6 1.9 fusion.34
  286.6 3.0 fusion.91
  289.6 3.2 select_subtract_fusion.2
  292.9 2.8 fusion.97
  295.7 2.1 select_subtract_fusion
  298.8 2.8 fusion.98
  301.6 3.5 fusion.42
  306.1 2.6 multiply_reduce_fusion.4
  309.8 2.9 fusion.38
  312.7 4.6 multiply_reduce_fusion.1
  317.3 3.3 fusion.66
  320.6 2.9 fusion.5
  323.5 4.4 fusion.63
  328.0 4.5 multiply_reduce_fusion.3
  332.5 2.8 fusion.64
  335.4 2.9 fusion.8
  338.4 3.1 fusion.61
  341.6 3.7 fusion.100
  345.4 1.9 convolution_add_fusion.1
  348.3 3.5 fusion.4
  351.8 2.0 fusion.30
  354.5 7.2 %multiply_reduce_fusion = (f32[]{:T(128)}, f32[512,512]{1,0:T(8,128)}) fusion(f32[]{:T(128)S(6)} %div.109, f32[512,512]{1,0:T(8,128)} %get-tuple-element.20, f32[512,512]{1,0:T(8,128)} %fusion.30, f32[512,512]{1,0:T(8,128)} %copy-done.20, f32[512,512]{1,0:T(8,128)} %copy-done.23), kind=kOutput, calls=%fused_computation.58 | convolution fusion | flops 1612709888 | bytes 5242888 | tf_op jit(solution)/shard_map/transpose(jvp())/dot_general | solution.py:19
  362.4 2.8 add_add_fusion
  365.2 2.5 copy.11
  367.7 3.1 fusion.13
  371.6 2.8 collective-permute-start.4
  374.5 3.2 fusion.99
  377.8 1.9 convolution_add_fusion.4
  380.7 3.5 fusion.7
  384.2 2.0 fusion.32
  386.9 7.3 %multiply_reduce_fusion.2 = (f32[]{:T(128)}, f32[512,512]{1,0:T(8,128)}) fusion(f32[]{:T(128)S(6)} %div.102, f32[512,512]{1,0:T(8,128)S(1)} %copy-done.4, f32[512,512]{1,0:T(8,128)} %fusion.32, f32[512,512]{1,0:T(8,128)} %copy-done.21, f32[512,512]{1,0:T(8,128)} %copy-done.22), kind=kOutput, calls=%fused_computation.60 | convolution fusion | flops 1612709888 | bytes 5242888 | tf_op jit(solution)/shard_map/transpose(jvp())/dot_general | solution.py:19
  394.8 1.8 add_add_fusion.1
  396.6 1.3 copy.10
  398.0 2.5 fusion.20
  401.6 2.3 convert_reduce_fusion
  404.4 1.3 collective-permute-start.5
  406.3 2.5 collective-permute-done.5
  409.6 1.3 collective-permute-start.6
  411.4 2.5 collective-permute-done.6
  414.7 1.3 collective-permute-start.7
  416.4 3.4 pad_maximum_fusion
  420.2 4.7 convolution_bitcast_fusion
  425.6 75.3 %all-reduce = (f32[512]{0:T(512)}, f32[3,512]{1,0:T(4,128)}) all-reduce(f32[512]{0:T(512)S(1)} %get-tuple-element.29, f32[3,512]{1,0:T(4,128)S(1)} %pad_maximum_fusion.2), channel_id=1, replica_groups=mesh['traj'=8,'tm'=16] {'traj','tm'}, use_global_device_ids=true, to_apply=%region_16.17 | all-reduce | flops 2048 | bytes 16384 | tf_op jit(solution)/shard_map/psum | solution.py:140
  500.8 107.6 %all-reduce.7.cloned.1.call-done = (f32[4096,512]{0,1:T(8,128)}, f32[3,1024,512]{2,1,0:T(8,128)}) async-done(((f32[4096,512]{0,1:T(8,128)}, f32[3,1024,512]{2,1,0:T(8,128)}), (f32[4096,512]{0,1:T(8,128)}, f32[3,1024,512]{2,1,0:T(8,128)})) %all-reduce.7.cloned.1.call-update) | async-done | bytes 14680080 | tf_op jit(solution)/shard_map/psum | solution.py:140
  608.4 8.9 %copy.12 = f32[4096,512]{1,0:T(8,128)} copy(f32[4096,512]{0,1:T(8,128)} %get-tuple-element.16) | data formatting | bytes 16777216
  617.3 6.2 copy.18
  (123 shorter events, 16.9 us)
Async XLA Ops:
  7.2 1.6 copy-start
  7.2 10.4 %copy-start.40 = (f32[3,512]{1,0:T(4,128)S(1)}, f32[3,512]{1,0:T(4,128)}, u32[]{:S(2)}) copy-start(f32[3,512]{1,0:T(4,128)} %param.9) | copy-start | bytes 18436
  7.2 262.9 %all-reduce.9.cloned.1.call-start = ((), (), s32[]{:S(2)}) async-start(), calls=%async_computation.1 | async-start | bytes 6291456 | tf_op jit(solution)/shard_map/psum | solution.py:85
  8.8 9.5 %copy-start.24 = (bf16[3,1024,512]{2,1,0:T(8,128)(2,1)S(1)}, bf16[3,1024,512]{2,1,0:T(8,128)(2,1)}, u32[]{:S(2)}) copy-start(bf16[3,1024,512]{2,1,0:T(8,128)(2,1)} %param.8) | copy-start | bytes 9437188
  13.2 12.0 %copy-start.29 = (bf16[256,512]{1,0:T(8,128)(2,1)}, bf16[256,512]{1,0:T(8,128)(2,1)S(1)}, u32[]{:S(2)}) copy-start(bf16[256,512]{1,0:T(8,128)(2,1)S(1)} %get-tuple-element.34) | copy-start | bytes 786436
  13.2 5.1 collective-permute-start
  19.5 5.6 copy-start.31
  19.5 4.3 collective-permute-start.1
  25.1 8.1 %copy-start.27 = (bf16[256,512]{1,0:T(8,128)(2,1)}, bf16[256,512]{1,0:T(8,128)(2,1)S(1)}, u32[]{:S(2)}) copy-start(bf16[256,512]{1,0:T(8,128)(2,1)S(1)} %get-tuple-element.38) | copy-start | bytes 786436
  25.1 4.3 collective-permute-start.2
  32.0 4.7 collective-permute-start.3
  33.3 86.0 %copy-start.7 = (bf16[240,512]{1,0:T(8,128)(2,1)}, bf16[240,512]{1,0:T(8,128)(2,1)S(1)}, u32[]{:S(2)}) copy-start(bf16[240,512]{1,0:T(8,128)(2,1)S(1)} %slice.110) | copy-start | bytes 737284
  119.3 489.1 %all-reduce.7.cloned.1.call-start = ((), (), s32[]{:S(2)}) async-start(), calls=%async_computation | async-start | bytes 29360128 | tf_op jit(solution)/shard_map/psum | solution.py:140
  272.9 3.5 copy-start.3
  275.4 1.0 copy-start.22
  282.1 4.4 copy-start.5
  284.6 1.9 copy-start.23
  289.6 6.1 copy-start.1
  289.6 6.1 copy-start.17
  292.9 4.9 copy-start.9
  297.8 1.0 copy-start.11
  301.6 4.5 copy-start.13
  305.2 1.0 copy-start.33
  308.7 1.0 copy-start.34
  312.7 4.6 copy-start.12
  317.3 3.3 copy-start.2
  328.0 4.6 copy-start.10
  341.6 3.8 copy-start.18
  341.6 3.8 copy-start.19
  341.6 3.8 copy-start.36
  345.4 2.9 copy-start.20
  345.4 2.9 copy-start.6
  370.8 0.8 copy-start.26
  371.6 29.9 %collective-permute-start.4 = (bf16[16,512]{1,0:T(8,128)(2,1)S(1)}, bf16[16,512]{1,0:T(8,128)(2,1)S(1)}, u32[]{:S(2)}, u32[]{:S(2)}) collective-permute-start(bf16[16,512]{1,0:T(8,128)(2,1)S(1)} %slice.161), channel_id=1, source_target_pairs={{0,1},{1,2},{2,3},{3,4},{4,5},{5,6},{6,7},{7,8},{8,9},{9,10},{10,1... | collective-permute-start | bytes 49160 | tf_op jit(solution)/shard_map/ppermute | solution.py:15
  374.5 3.3 copy-start.15
  374.5 3.3 copy-start.16
  374.5 3.3 copy-start.35
  377.8 2.9 copy-start.21
  377.8 2.9 copy-start.4
  398.0 3.6 copy-start.8
  398.0 3.6 copy-start.14
  398.0 6.0 copy-start.25
  401.6 4.2 copy-start.28
  403.9 4.9 copy-start.38
  404.4 4.4 collective-permute-start.5
  406.2 4.7 copy-start.32
  409.1 4.8 copy-start.37
  409.6 4.4 collective-permute-start.6
  411.3 4.6 copy-start.30
  414.7 5.3 collective-permute-start.7
  416.4 3.5 copy-start.39
Sparse Core Ops, SparseCore 0:
  119.5 150.6 all-reduce.8
  425.0 183.3 all-reduce.6
where the time goes:
time: 638 us; the launch traced here: 632 us
  waiting for transfers between devices  269 us (42%)
  blocking collectives  151 us (24%)
  matrix products  132 us (21%)
  local copies, waits for them, and re-layouts  25.8 us (4%)
  between operations  21.2 us (3%)
  starting transfers between devices  19.8 us (3%)
  other arithmetic  13.2 us (2%)
    psum x1, waiting for transfers between devices, per_device(): lax.psum((gram_hi(centred_early, centred_early), gram_hi(centred_early, c...  151 us
    dot_general x36, matrix products, matmul_hi(): jnp.dot(first_mat, second_mat, precision=lax.Precision.HIGHEST, preferred...  108 us
    psum x1, waiting for transfers between devices, per_device(): lax.psum((local_w_in, local_b_in, stacked_w, stacked_b), ('traj', 'tm'))  108 us
    psum x1, blocking collectives, per_device(): lax.psum((jnp.sum(early_rows, axis=0), jnp.sum(later_rows, axis=0)), ('tr...  75.7 us
    psum x1, blocking collectives, per_device(): lax.psum((local_w_in, local_b_in, stacked_w, stacked_b), ('traj', 'tm'))  75.3 us
    unnamed x84, local copies, waits for them, and re-layouts  20.6 us
    ppermute x8, starting transfers between devices, from_behind(): lax.ppermute(value, axis, [(source, source + steps) for source in range(i...  19.5 us
  transfers between devices with their start and end apart: 10, of which 8 were waited for; matrix products, arithmetic and copies ran while one was open for 5% of the time, Pallas kernels for 0%

commit v1 on v0

--- a/solution.py
+++ b/solution.py
@@ -79,7 +79,9 @@
     early_rows = hidden.astype(jnp.float32) * pair_mask
     later_rows = jnp.concatenate([hidden[LAG:], upcoming], axis=0).astype(jnp.float32) * pair_mask
     pair_count = lax.axis_size("traj") * (row_count * segments - LAG)
-    totals = lax.psum((jnp.sum(early_rows, axis=0), jnp.sum(later_rows, axis=0)), ("traj", "tm"))
+    totals = lax.psum(
+        lax.psum((jnp.sum(early_rows, axis=0), jnp.sum(later_rows, axis=0)), "tm"), "traj"
+    )
     centred_early = (early_rows - totals[0] / pair_count) * pair_mask
     centred_later = (later_rows - totals[1] / pair_count) * pair_mask
     moments = lax.psum(

time: 638 us -> 618 us (0.969)
  blocking collectives: 151 us -> 133 us
    psum x1 -> x2, blocking collectives: 75.7 us -> 58.2 us  [the longest x1 34.5 us: per_device(): lax.psum((jnp.sum(early_rows, axis=0), jnp.sum(later_rows, axis=0)), 'tm')]
where the time goes in v1:
time: 618 us; the launch traced here: 612 us
  waiting for transfers between devices  266 us (43%)
  blocking collectives  133 us (22%)
  matrix products  132 us (21%)
  local copies, waits for them, and re-layouts  25.8 us (4%)
  between operations  21.2 us (3%)
  starting transfers between devices  19.8 us (3%)
  other arithmetic  13.2 us (2%)
    psum x1, waiting for transfers between devices, per_device(): lax.psum((gram_hi(centred_early, centred_early), gram_hi(centred_early, c...  148 us
    dot_general x36, matrix products, matmul_hi(): jnp.dot(first_mat, second_mat, precision=lax.Precision.HIGHEST, preferred...  108 us
    psum x1, waiting for transfers between devices, per_device(): lax.psum((local_w_in, local_b_in, stacked_w, stacked_b), ('traj', 'tm'))  108 us
    psum x1, blocking collectives, per_device(): lax.psum((local_w_in, local_b_in, stacked_w, stacked_b), ('traj', 'tm'))  75.3 us
    psum x1, blocking collectives, per_device(): lax.psum((jnp.sum(early_rows, axis=0), jnp.sum(later_rows, axis=0)), 'tm')  34.5 us
    psum x1, blocking collectives, per_device(): lax.psum(lax.psum((jnp.sum(early_rows, axis=0), jnp.sum(later_rows, axis=...  23.7 us
    unnamed x84, local copies, waits for them, and re-layouts  20.6 us
    ppermute x8, starting transfers between devices, from_behind(): lax.ppermute(value, axis, [(source, source + steps) for source in range(i...  19.5 us
  transfers between devices with their start and end apart: 10, of which 8 were waited for; matrix products, arithmetic and copies ran while one was open for 5% of the time, Pallas kernels for 0%

profile of v1, /device:TPU:1, one launch (start us, length us, event | category | flops | bytes accessed | tf_op | source)
XLA Modules:
  0.0 611.5 jit_solution(11813682518884617447)
XLA Ops:
  7.2 1.5 copy-done
  8.8 4.4 fusion.96
  13.2 4.4 collective-permute-start
  19.6 3.6 collective-permute-start.1
  25.1 3.6 collective-permute-start.2
  29.5 2.5 add_convert_fusion
  33.3 3.4 collective-permute-done.3
  36.9 34.5 %all-reduce.3 = (f32[512]{0:T(512)S(1)}, f32[512]{0:T(512)S(1)}) all-reduce(f32[512]{0:T(512)S(1)} %get-tuple-element.11, f32[512]{0:T(512)S(1)} %get-tuple-element.10), channel_id=1, replica_groups=mesh['traj'=8,'tm'=16] {'tm'}, use_global_device_ids=true, to_apply=%region_6.7 | all-reduce | flops 1024 | bytes 8192 | tf_op jit(solution)/shard_map/psum | solution.py:83
  71.4 23.7 %all-reduce.4 = (f32[512]{0:T(512)S(1)}, f32[512]{0:T(512)S(1)}) all-reduce(f32[512]{0:T(512)S(1)} %get-tuple-element.19, f32[512]{0:T(512)S(1)} %get-tuple-element.20), channel_id=1, replica_groups=mesh['traj'=8,'tm'=16] {'traj'}, use_global_device_ids=true, to_apply=%region_7.8 | all-reduce | flops 1024 | bytes 8192 | tf_op jit(solution)/shard_map/psum | solution.py:82
  95.1 2.2 fusion.62
  97.3 2.2 fusion.57
  99.6 2.2 fusion.56
  102.0 148.0 %all-reduce.10.cloned.1.call-done = (f32[512,512]{1,0:T(8,128)}, f32[512,512]{1,0:T(8,128)}, f32[512,512]{1,0:T(8,128)}) async-done(((f32[512,512]{1,0:T(8,128)}, f32[512,512]{1,0:T(8,128)}, f32[512,512]{1,0:T(8,128)}), (f32[512,512]{1,0:T(8,128)}, f32[512,512]{1,0:T(8,128)}, f32[512,512]{1,0:T(8,128)})) %all-reduce.10.cloned.1.call-update) | async-done | bytes 3145744 | tf_op jit(solution)/shard_map/psum | solution.py:87
  250.0 2.1 multiply_reduce_fusion.6
  252.8 2.5 select_subtract_fusion.3
  256.3 2.9 fusion.90
  259.3 2.1 multiply_reduce_fusion.5
  262.1 2.5 select_subtract_fusion.1
  264.5 1.9 fusion.34
  266.5 3.0 fusion.91
  269.5 3.2 select_subtract_fusion.2
  272.8 2.8 fusion.97
  275.6 2.1 select_subtract_fusion
  278.7 2.8 fusion.98
  281.5 3.5 fusion.42
  286.0 2.6 multiply_reduce_fusion.4
  289.7 2.9 fusion.38
  292.6 4.6 multiply_reduce_fusion.1
  297.2 3.3 fusion.66
  300.5 2.9 fusion.5
  303.4 4.4 fusion.63
  307.9 4.5 multiply_reduce_fusion.3
  312.4 2.8 fusion.64
  315.3 2.9 fusion.8
  318.3 3.2 fusion.61
  321.5 3.7 fusion.100
  325.3 1.9 convolution_add_fusion.1
  328.2 3.5 fusion.4
  331.7 2.0 fusion.30
  334.4 7.2 %multiply_reduce_fusion = (f32[]{:T(128)}, f32[512,512]{1,0:T(8,128)}) fusion(f32[]{:T(128)S(6)} %div.109, f32[512,512]{1,0:T(8,128)} %get-tuple-element.18, f32[512,512]{1,0:T(8,128)} %fusion.30, f32[512,512]{1,0:T(8,128)} %copy-done.20, f32[512,512]{1,0:T(8,128)} %copy-done.23), kind=kOutput, calls=%fused_computation.58 | convolution fusion | flops 1612709888 | bytes 5242888 | tf_op jit(solution)/shard_map/transpose(jvp())/dot_general | solution.py:19
  342.3 2.8 add_add_fusion
  345.0 2.6 copy.11
  347.6 3.1 fusion.13
  351.5 2.8 collective-permute-start.4
  354.4 3.2 fusion.99
  357.7 1.9 convolution_add_fusion.4
  360.5 3.5 fusion.7
  364.0 2.0 fusion.32
  366.7 7.3 %multiply_reduce_fusion.2 = (f32[]{:T(128)}, f32[512,512]{1,0:T(8,128)}) fusion(f32[]{:T(128)S(6)} %div.102, f32[512,512]{1,0:T(8,128)S(1)} %copy-done.4, f32[512,512]{1,0:T(8,128)} %fusion.32, f32[512,512]{1,0:T(8,128)} %copy-done.21, f32[512,512]{1,0:T(8,128)} %copy-done.22), kind=kOutput, calls=%fused_computation.60 | convolution fusion | flops 1612709888 | bytes 5242888 | tf_op jit(solution)/shard_map/transpose(jvp())/dot_general | solution.py:19
  374.7 1.8 add_add_fusion.1
  376.5 1.3 copy.10
  377.9 2.5 fusion.20
  381.5 2.3 convert_reduce_fusion
  384.3 1.3 collective-permute-start.5
  386.2 2.5 collective-permute-done.5
  389.4 1.3 collective-permute-start.6
  391.3 2.5 collective-permute-done.6
  394.5 1.3 collective-permute-start.7
  396.3 3.4 pad_maximum_fusion
  400.1 4.7 convolution_bitcast_fusion
  405.5 75.3 %all-reduce = (f32[512]{0:T(512)}, f32[3,512]{1,0:T(4,128)}) all-reduce(f32[512]{0:T(512)S(1)} %get-tuple-element.31, f32[3,512]{1,0:T(4,128)S(1)} %pad_maximum_fusion.2), channel_id=1, replica_groups=mesh['traj'=8,'tm'=16] {'traj','tm'}, use_global_device_ids=true, to_apply=%region_18.19 | all-reduce | flops 2048 | bytes 16384 | tf_op jit(solution)/shard_map/psum | solution.py:142
  480.7 107.5 %all-reduce.8.cloned.1.call-done = (f32[4096,512]{0,1:T(8,128)}, f32[3,1024,512]{2,1,0:T(8,128)}) async-done(((f32[4096,512]{0,1:T(8,128)}, f32[3,1024,512]{2,1,0:T(8,128)}), (f32[4096,512]{0,1:T(8,128)}, f32[3,1024,512]{2,1,0:T(8,128)})) %all-reduce.8.cloned.1.call-update) | async-done | bytes 14680080 | tf_op jit(solution)/shard_map/psum | solution.py:142
  588.3 8.9 %copy.12 = f32[4096,512]{1,0:T(8,128)} copy(f32[4096,512]{0,1:T(8,128)} %get-tuple-element.14) | data formatting | bytes 16777216
  597.2 6.2 %copy.18 = f32[3,1024,512]{2,1,0:T(8,128)} copy(f32[3,1024,512]{2,1,0:T(8,128)} %get-tuple-element.60) | data formatting | bytes 12582912
  (124 shorter events, 18.2 us)
Async XLA Ops:
  7.2 1.6 copy-start
  7.2 10.4 %copy-start.40 = (f32[3,512]{1,0:T(4,128)S(1)}, f32[3,512]{1,0:T(4,128)}, u32[]{:S(2)}) copy-start(f32[3,512]{1,0:T(4,128)} %param.9) | copy-start | bytes 18436
  7.2 242.8 %all-reduce.10.cloned.1.call-start = ((), (), s32[]{:S(2)}) async-start(), calls=%async_computation.1 | async-start | bytes 6291456 | tf_op jit(solution)/shard_map/psum | solution.py:87
  8.8 9.5 %copy-start.24 = (bf16[3,1024,512]{2,1,0:T(8,128)(2,1)S(1)}, bf16[3,1024,512]{2,1,0:T(8,128)(2,1)}, u32[]{:S(2)}) copy-start(bf16[3,1024,512]{2,1,0:T(8,128)(2,1)} %param.8) | copy-start | bytes 9437188
  13.2 12.0 %copy-start.29 = (bf16[256,512]{1,0:T(8,128)(2,1)}, bf16[256,512]{1,0:T(8,128)(2,1)S(1)}, u32[]{:S(2)}) copy-start(bf16[256,512]{1,0:T(8,128)(2,1)S(1)} %get-tuple-element.36) | copy-start | bytes 786436
  13.2 5.1 collective-permute-start
  19.5 5.6 copy-start.31
  19.6 4.3 collective-permute-start.1
  25.1 8.2 %copy-start.27 = (bf16[256,512]{1,0:T(8,128)(2,1)}, bf16[256,512]{1,0:T(8,128)(2,1)S(1)}, u32[]{:S(2)}) copy-start(bf16[256,512]{1,0:T(8,128)(2,1)S(1)} %get-tuple-element.40) | copy-start | bytes 786436
  25.1 4.3 collective-permute-start.2
  32.0 4.7 collective-permute-start.3
  33.3 68.5 %copy-start.7 = (bf16[240,512]{1,0:T(8,128)(2,1)}, bf16[240,512]{1,0:T(8,128)(2,1)S(1)}, u32[]{:S(2)}) copy-start(bf16[240,512]{1,0:T(8,128)(2,1)S(1)} %slice.110) | copy-start | bytes 737284
  101.8 486.4 %all-reduce.8.cloned.1.call-start = ((), (), s32[]{:S(2)}) async-start(), calls=%async_computation | async-start | bytes 29360128 | tf_op jit(solution)/shard_map/psum | solution.py:142
  252.8 3.5 copy-start.3
  255.3 1.0 copy-start.22
  262.0 4.4 copy-start.5
  264.5 2.0 copy-start.23
  269.5 6.1 copy-start.1
  269.5 6.1 copy-start.17
  272.8 4.9 copy-start.9
  277.7 1.0 copy-start.11
  281.5 4.5 copy-start.13
  285.0 1.0 copy-start.33
  288.6 1.0 copy-start.34
  292.6 4.6 copy-start.12
  297.2 3.3 copy-start.2
  307.9 4.6 copy-start.10
  321.5 3.8 copy-start.18
  321.5 3.8 copy-start.19
  321.5 3.8 copy-start.36
  325.3 2.9 copy-start.20
  325.3 2.9 copy-start.6
  350.7 0.8 copy-start.26
  351.5 29.9 %collective-permute-start.4 = (bf16[16,512]{1,0:T(8,128)(2,1)S(1)}, bf16[16,512]{1,0:T(8,128)(2,1)S(1)}, u32[]{:S(2)}, u32[]{:S(2)}) collective-permute-start(bf16[16,512]{1,0:T(8,128)(2,1)S(1)} %slice.161), channel_id=1, source_target_pairs={{0,1},{1,2},{2,3},{3,4},{4,5},{5,6},{6,7},{7,8},{8,9},{9,10},{10,1... | collective-permute-start | bytes 49160 | tf_op jit(solution)/shard_map/ppermute | solution.py:15
  354.4 3.3 copy-start.15
  354.4 3.3 copy-start.16
  354.4 3.3 copy-start.35
  357.6 2.9 copy-start.21
  357.7 2.9 copy-start.4
  377.8 3.6 copy-start.8
  377.8 3.6 copy-start.14
  377.8 6.0 copy-start.25
  381.4 4.2 copy-start.28
  383.8 4.9 copy-start.38
  384.3 4.4 collective-permute-start.5
  386.1 4.7 copy-start.32
  389.0 4.8 copy-start.37
  389.4 4.4 collective-permute-start.6
  391.2 4.6 copy-start.30
  394.5 5.3 collective-permute-start.7
  396.3 3.5 copy-start.39
Sparse Core Ops, SparseCore 0:
  101.9 148.0 all-reduce.9
  404.9 183.2 all-reduce.7
